TPU v7x, 128 devices: a whole 4x4x4 slice. The times are simulated.
128 devices in a mesh: space: 32 (over y, x_hi, z), species: 4 (over x_lo, core).
Axes of the slice: x: 4 (x_hi: 2, x_lo: 2; x = x_hi * 2 + x_lo), y: 4, z: 4, core: 2. Of those that a mesh axis runs over, the one named last changes fastest.
Arguments:
- effects: float32 [192, 256, 2048], P('space', None, 'species'), may hold values from -1.2 to 1.2
- kappa_sq: float32 [192, 256], P('space'), may hold values from 0.1 to 2
- growth: float32 [192, 256, 128], P('space'), may hold values from -6 to 6
- tree_species: int32 [192, 256, 128], P('space'), may hold values from 0 to 2047
- tree_counts: int32 [192, 256], P('space'), may hold values from 1 to 128, as said below
- noise_precision: float32 [2048], P('species'), may hold values from 0.5 to 4
- species_precision: bfloat16 [2048, 2048], P(None, 'species'), as said below
Outputs:
- grad_effects: float32 [192, 256, 2048], P('space', None, 'species')
- gram: float32 [2048, 2048], P('space', 'species')
Inputs may be any that keep to these rules, and one draw needn't show every extreme that they name: `tree_counts`: some plot has 128 live trees. species_precision is symmetric.
All inputs are finite; a program needn't handle non-finite values.
Results may differ from a plain program's by a relative error of at most 0.0029.
Values may be sent and summed in bfloat16 or wider, within the bound.
A program may use at most 128 MiB of HBM per device.

v0:
```python
import jax
import jax.numpy as jnp
from jax import lax
from jax.experimental import pallas as pl
from jax.experimental.pallas import tpu as pltpu
from jax.sharding import PartitionSpec as P

MESH = pl.DeviceIdType.MESH
BF = jnp.bfloat16
F32 = jnp.float32
R, C, W, T = 6, 256, 512, 128
NP = R * C
GROUP = 32
CHUNKS = ((2 * C, C // 2), (2 * C + C // 2, C // 2), (3 * C, C), (C, C), (4 * C, C), (0, C), (5 * C, C))
NC = len(CHUNKS)


def kernel(
    eff_in, kap, growth_in, species_in, counts, noise, prec_in,
    out_hbm, gram,
    eff, growth, species, prec, out,
    near, far_out, far_in, relayed, kap_up, kap_dn, tmp, kap_b, cnt_b, first, spat, eff_t, sums,
    part, late, rz, ry, mid0, mid1, rz2, ry2, held, fin,
    halo_s, halo_r, relay_s, relay_r, ex_s, ex_r, gz_s, gz_r, gy_s, gy_r, g2y_s, g2y_r, g2z_s, g2z_r, last_s, last_r, in_sem, out_sem,
):
    sp, me = lax.axis_index("space"), lax.axis_index("species")
    z, xh, y = sp % 4, (sp // 4) % 2, sp // 8
    up, dn = (sp + 31) % 32, (sp + 1) % 32
    sib = (me // 2) * 2 + (me + 1) % 2
    far = (me + 2) % 4

    def at(yy, hh, zz):
        return (yy * 2 + hh) * 4 + zz

    def dev(space, spec):
        return {"space": space, "species": spec}

    def block(k):
        return ((me // 2 + k // 2) % 2) * 2 + (me % 2 + k % 2) % 2

    moved = y != me

    def remote(src, dst, ssem, rsem, to):
        return pltpu.make_async_remote_copy(
            src_ref=src, dst_ref=dst, send_sem=ssem, recv_sem=rsem, device_id=to, device_id_type=MESH
        )

    loads = [pltpu.make_async_copy(eff_in.at[pl.ds(r * C, C)], eff.at[pl.ds(r * C, C)], in_sem.at[r]) for r in range(R)]
    for r in (1, 4, 2, 3, 0, 5):
        loads[r].start()
    load_species = pltpu.make_async_copy(species_in, species, in_sem.at[R])
    load_growth = pltpu.make_async_copy(growth_in, growth, in_sem.at[R + 1])
    load_prec = pltpu.make_async_copy(prec_in, prec, in_sem.at[R + 2])
    load_species.start()
    load_growth.start()
    load_prec.start()

    barrier = pltpu.get_barrier_semaphore()
    peers = [dev(up, me), dev(dn, me), dev(sp, sib), dev(sp, far)]
    peers += [dev(at(y, xh, (z + d) % 4), me) for d in (1, 2, 3)]
    peers += [dev(at((y + d) % 4, xh, z), me) for d in (1, 2, 3)]
    peers += [dev(at((y + d) % 4, h, z), y) for d in (1, 2, 3) for h in (0, 1)]
    peers += [dev(at(y, 1 - xh, z), y)]
    for peer in peers:
        pl.semaphore_signal(barrier, inc=1, device_id=peer, device_id_type=MESH)

    @pl.when(moved)
    def _():
        pl.semaphore_signal(barrier, inc=1, device_id=dev(sp, y), device_id_type=MESH)

    outer = (z == 0, z == 3)
    inner = (z == 1, z == 2)
    for i in range(2):

        @pl.when(outer[i])
        def _():
            pl.semaphore_signal(barrier, inc=1, device_id=dev((dn, up)[i], far), device_id_type=MESH)

    is_inner = jnp.logical_or(z == 1, z == 2)

    tmp[...] = jnp.zeros_like(tmp)
    tmp[0:R, :] = kap[...]
    kap_cols = tmp[...].T
    for r in range(R):
        kap_b[r + 1] = jnp.broadcast_to(kap_cols[:, r : r + 1], (C, T)) + 4.0

    pl.semaphore_wait(barrier, len(peers) + moved.astype(jnp.int32) + is_inner.astype(jnp.int32))

    def far_row(i):
        return remote(
            far_out.at[i], far_in.at[i], halo_s.at[4 + i], halo_r.at[4 + i], dev(up if i == 0 else dn, me)
        )

    halos = [
        remote(eff_in.at[pl.ds(0, C)], near.at[1], halo_s.at[0], halo_r.at[0], dev(up, me)),
        remote(eff_in.at[pl.ds(5 * C, C)], near.at[0], halo_s.at[1], halo_r.at[1], dev(dn, me)),
        remote(kap, kap_dn, halo_s.at[2], halo_r.at[2], dev(up, me)),
        remote(kap, kap_up, halo_s.at[3], halo_r.at[3], dev(dn, me)),
        far_row(0),
        far_row(1),
    ]
    for copy in halos[:4]:
        copy.start()
    for i, r in enumerate((1, 4)):
        loads[r].wait()
        far_out[i] = eff[r * C : (r + 1) * C, :].astype(BF)
        halos[4 + i].start()

    for r in (2, 3, 0, 5):
        loads[r].wait()

    def erow(r):
        if 0 <= r < R:
            return eff.at[pl.ds(r * C, C)]
        return {-2: far_in.at[1], -1: near.at[0], 6: near.at[1], 7: far_in.at[0]}[r]

    edge = lax.broadcasted_iota(jnp.int32, (C, T), 0)

    def stencil(centre, above, below, kappa):
        left = jnp.where(edge == 0, 0.0, pltpu.roll(centre, 1, 0))
        right = jnp.where(edge == C - 1, 0.0, pltpu.roll(centre, C - 1, 0))
        return kappa * centre - (below + above + right + left)

    def first_row(r):
        def body(c, carry):
            cs = pl.ds(pl.multiple_of(c * T, T), T)
            first[r + 1, :, cs] = stencil(
                erow(r)[:, cs], erow(r - 1)[:, cs].astype(F32), erow(r + 1)[:, cs].astype(F32), kap_b[r + 1]
            )
            return carry

        lax.fori_loop(0, W // T, body, 0)

    def spat_row(r):
        def body(c, carry):
            cs = pl.ds(pl.multiple_of(c * T, T), T)
            s = stencil(first[r + 1, :, cs], first[r, :, cs], first[r + 2, :, cs], kap_b[r + 1])
            spat[0, r * C : (r + 1) * C, cs] = s.astype(BF)
            return carry

        lax.fori_loop(0, W // T, body, 0)

    def piece(k, i):
        return spat.at[k, pl.ds(*CHUNKS[i])]

    def to_sib(i):
        return remote(piece(0, i), piece(1, i), ex_s.at[0, i], ex_r.at[0, i], dev(sp, sib))

    def to_far(i):
        return remote(piece(0, i), piece(2, i), ex_s.at[1, i], ex_r.at[1, i], dev(sp, far))

    def on(i):
        return remote(piece(2, i), piece(3, i), ex_s.at[2, i], ex_r.at[2, i], dev(sp, sib))

    def relay(j):
        return relayed.at[pl.ds(CHUNKS[j][0] - 2 * C, CHUNKS[j][1])]

    def to_relay(i, j):
        return remote(piece(0, j), relay(j), ex_s.at[1, j], relay_r.at[j], dev((dn, up)[i], me))

    def from_relay(i, j):
        return remote(relay(j), piece(2, j), relay_s.at[j], ex_r.at[1, j], dev((up, dn)[i], far))

    def pass_on(j):
        for i in range(2):

            @pl.when(inner[i])
            def _():
                to_relay(i, j).wait_recv()
                from_relay(i, j).start()

    def send(*chunks):
        for i in chunks:
            if i < 2:
                for t in range(2):

                    @pl.when(outer[t])
                    def _():
                        to_relay(t, i).start()

                @pl.when(is_inner)
                def _():
                    to_far(i).start()

            else:
                to_far(i).start()
            to_sib(i).start()

    lane = lax.broadcasted_iota(jnp.int32, (8, T), 1)
    low_iota = lax.broadcasted_iota(jnp.int32, (T, T), 0)
    sub = lax.broadcasted_iota(jnp.int32, (8, T), 0)
    nothing = jnp.zeros((8, T), F32)

    def trees(row_lo, row_hi):
        def step(g, r):
            start = r * C + g * GROUP
            for q in range(GROUP // 8):
                rows = pl.ds(pl.multiple_of(start + q * 8, 8), 8)
                ids = species[rows, :]
                live = lane < cnt_b[rows, :]
                high = jnp.where(live, lax.shift_right_arithmetic(ids, 7) - 4 * me, -1)
                low = ids & 127
                value = growth[rows, :].astype(BF).astype(F32)

                def left_side(p):
                    chosen = jnp.broadcast_to(high[p : p + 1, :], (8, T)) == (sub & 3)
                    held_value = jnp.where(sub < 4, jnp.broadcast_to(value[p : p + 1, :], (8, T)), 1.0)
                    return jnp.where(chosen, held_value, 0.0)

                def right_side(p):
                    same = jnp.broadcast_to(low[p : p + 1, :], (T, T)) == low_iota
                    return jnp.where(same, 1.0, 0.0).astype(BF)

                for p in range(0, 8, 2):
                    a = jnp.concatenate(
                        [
                            jnp.concatenate([left_side(p), nothing], 1),
                            jnp.concatenate([nothing, left_side(p + 1)], 1),
                        ],
                        0,
                    ).astype(BF)
                    b = jnp.concatenate([right_side(p), right_side(p + 1)], 1)
                    both = lax.dot_general(a, b, (((1,), (1,)), ((), ())), preferred_element_type=F32)
                    for j in range(2):
                        sums[pl.ds(g * GROUP + q * 8 + p + j, 8, stride=C), :] = both[j * 8 : (j + 1) * 8, :]
            return r

        def whole(r, carry):
            lax.fori_loop(0, C // GROUP, step, r)
            rows = pl.ds(pl.multiple_of(r * C, C), C)
            for h in range(4):
                cs = slice(h * T, (h + 1) * T)
                total = sums[h * C : (h + 1) * C, :]
                tally = sums[(h + 4) * C : (h + 5) * C, :]
                out[rows, cs] = noise[:, cs] * (total - tally * eff[rows, cs])
            return carry

        lax.fori_loop(row_lo, row_hi, whole, 0)

    def prior(ks, start, size, steps):
        def body(i, carry):
            rows = pl.ds(pl.multiple_of(start + i * size, 256), size)
            total = None
            for k in ks:
                q = prec[pl.ds(pl.multiple_of(block(k) * W, W), W), :]
                term = jnp.dot(spat[k, rows, :], q, preferred_element_type=F32)
                total = term if total is None else total + term
            out[rows, :] = out[rows, :] - total
            return carry

        lax.fori_loop(0, steps, body, 0)

    def store(i, start, size):
        rows = pl.ds(start, size)
        return pltpu.make_async_copy(out.at[rows], out_hbm.at[rows], out_sem.at[i])

    def gram_block(k):
        def body(i, carry):
            cs = pl.ds(pl.multiple_of(i * 256, 256), 256)
            part[k, :, cs] = jnp.dot(eff_t[...], spat[k, :, cs], preferred_element_type=F32).astype(BF)
            return carry

        lax.fori_loop(0, W // 256, body, 0)

    def gram_rows(k, starts, size, cs):
        total = None
        for r in starts:
            rows = slice(r * C, (r + size) * C)
            term = jnp.dot(eff_t[:, rows], spat[k, rows, cs], preferred_element_type=F32)
            total = term if total is None else total + term
        return total

    def gram_early(k):
        def body(i, carry):
            cs = pl.ds(pl.multiple_of(i * 256, 256), 256)
            late[k - 2, :, cs] = gram_rows(k, (1,), 1, cs) + gram_rows(k, (3,), 2, cs)
            return carry

        lax.fori_loop(0, W // 256, body, 0)

    def gram_late(k):
        def body(i, carry):
            cs = pl.ds(pl.multiple_of(i * 256, 256), 256)
            total = late[k - 2, :, cs] + gram_rows(k, (0, 2, 5), 1, cs)
            part[k, :, cs] = total.astype(BF)
            return carry

        lax.fori_loop(0, W // 256, body, 0)

    def z_peer(d):
        return dev(at(y, xh, (z + d) % 4), me)

    def gz(k, d):
        src = part.at[k, pl.ds(pl.multiple_of(((z + d) % 4) * 64, 64), 64)]
        return remote(src, rz.at[d - 1, k], gz_s.at[k, d - 1], gz_r.at[k, d - 1], z_peer(d))

    def y_peer(d):
        return dev(at((y + d) % 4, xh, z), me)

    def gy(k, d):
        src = part.at[k, pl.ds(256, 256), pl.ds(pl.multiple_of(((y + d) % 4) * T, T), T)]
        return remote(src, ry.at[d - 1, k], gy_s.at[k, d - 1], gy_r.at[k, d - 1], y_peer(d))

    def gram_send(k):
        for d in (1, 2, 3):
            gz(k, d).start()
            gy(k, d).start()

    def g2y(p, d):
        return remote(
            mid0.at[p, (y + d) % 4], ry2.at[p, d - 1], g2y_s.at[p, d - 1], g2y_r.at[p, d - 1], y_peer(d)
        )

    def g2z(p, d):
        src = mid1.at[p, pl.ds(pl.multiple_of(((z + d) % 4) * 64, 64), 64)]
        return remote(src, rz2.at[p, d - 1], g2z_s.at[p, d - 1], g2z_r.at[p, d - 1], z_peer(d))

    own_rows = pl.ds(pl.multiple_of(z * 64, 64), 64)
    own_cols = pl.ds(pl.multiple_of(y * T, T), T)

    def first_sums(p):
        for k in (2 * p, 2 * p + 1):
            cs = slice((k % 2) * T, (k % 2 + 1) * T)
            for d in (1, 2, 3):
                gz(k, d).wait_recv()
            total = part[k, own_rows, :].astype(F32)
            for d in (1, 2, 3):
                total = total + rz[d - 1, k].astype(F32)
            for q in range(4):
                mid0[p, q, :, cs] = total[:, q * T : (q + 1) * T].astype(BF)
        for d in (1, 2, 3):
            g2y(p, d).start()
        for k in (2 * p, 2 * p + 1):
            cs = slice((k % 2) * T, (k % 2 + 1) * T)
            for d in (1, 2, 3):
                gy(k, d).wait_recv()
            total = part[k, 256:512, own_cols].astype(F32)
            for d in (1, 2, 3):
                total = total + ry[d - 1, k].astype(F32)
            mid1[p, :, cs] = total.astype(BF)
        for d in (1, 2, 3):
            g2z(p, d).start()

    def to_result(h, k):
        return remote(
            held.at[h, :, pl.ds(k * T, T)],
            fin.at[xh, :, own_cols],
            last_s.at[h, k],
            last_r.at[xh, y],
            dev(at(me, h, z), block(k)),
        )

    def leaves(h):
        return jnp.logical_or(h != xh, moved)

    def results(p, h):
        for k in (2 * p, 2 * p + 1):
            if k:
                to_result(h, k).start()
            else:

                @pl.when(leaves(h))
                def _():
                    to_result(h, 0).start()

                @pl.when(jnp.logical_not(leaves(h)))
                def _():
                    fin[xh, :, own_cols] = held[h, :, 0:T]

    def arrived(h, q):
        return remote(
            held.at[0, :, pl.ds(0, T)], fin.at[h, :, pl.ds(q * T, T)], last_s.at[0, 0], last_r.at[h, q], dev(sp, sib)
        )

    def second_sums(p):
        cs = slice(p * 2 * T, (p + 1) * 2 * T)
        for d in (1, 2, 3):
            g2y(p, d).wait_recv()
        total = mid0[p, y].astype(F32)
        for d in (1, 2, 3):
            total = total + ry2[p, d - 1].astype(F32)
        held[0, :, cs] = total.astype(BF)
        results(p, 0)
        for d in (1, 2, 3):
            g2z(p, d).wait_recv()
        total = mid1[p, own_rows, :].astype(F32)
        for d in (1, 2, 3):
            total = total + rz2[p, d - 1].astype(F32)
        held[1, :, cs] = total.astype(BF)
        results(p, 1)

    for r in (1, 2, 3, 4):
        first_row(r)
    spat_row(2)
    spat_row(3)
    send(2, 0, 1)
    tmp[0:R, :] = counts[...].astype(F32)
    cnt_cols = tmp[...].T
    for r in range(R):
        cnt_b[r * C : (r + 1) * C, :] = jnp.broadcast_to(cnt_cols[:, r : r + 1], (C, T)).astype(jnp.int32)
    load_species.wait()
    load_growth.wait()
    trees(0, 2)

    for i in range(4):
        halos[i].wait_recv()
    tmp[0:1, :] = kap_up[R - 1 : R, :]
    tmp[1:2, :] = kap_dn[0:1, :]
    kap_edge = tmp[...].T
    kap_b[0] = jnp.broadcast_to(kap_edge[:, 0:1], (C, T)) + 4.0
    kap_b[R + 1] = jnp.broadcast_to(kap_edge[:, 1:2], (C, T)) + 4.0

    @pl.when(sp == 0)
    def _():
        near[0] = jnp.zeros((C, W), F32)

    @pl.when(sp == 31)
    def _():
        near[1] = jnp.zeros((C, W), F32)

    first_row(0)
    first_row(5)
    spat_row(1)
    spat_row(4)
    send(3, 4)
    trees(2, 3)
    pass_on(0)
    pass_on(1)
    trees(3, 4)

    halos[4].wait_recv()
    halos[5].wait_recv()
    first_row(-1)
    first_row(6)

    @pl.when(sp == 0)
    def _():
        first[0] = jnp.zeros((C, W), F32)

    @pl.when(sp == 31)
    def _():
        first[R + 1] = jnp.zeros((C, W), F32)

    spat_row(0)
    spat_row(5)
    send(5, 6)

    for r in range(R):
        eff_t[:, r * C : (r + 1) * C] = eff[r * C : (r + 1) * C, :].T.astype(BF)
    gram_block(0)
    gram_send(0)
    for i in range(NC):
        to_sib(i).wait_recv()
    gram_block(1)
    gram_send(1)
    trees(4, 6)
    load_prec.wait()
    prior((0, 1), 0, 512, 3)

    for i in (2, 3, 4):
        to_far(i).wait_recv()
        on(i).start()
    first_sums(0)
    gram_early(2)
    for i in (2, 3, 4):
        on(i).wait_recv()
    gram_early(3)
    prior((2, 3), C, C, 1)
    prior((2, 3), 4 * C, C, 1)
    store(0, C, C).start()
    store(1, 4 * C, C).start()
    second_sums(0)

    for i in (5, 6, 0, 1):
        to_far(i).wait_recv()
        on(i).start()
    gram_late(2)
    gram_send(2)
    for i in (5, 6, 0, 1):
        on(i).wait_recv()
    gram_late(3)
    gram_send(3)
    prior((2, 3), 2 * C, 2 * C, 1)
    prior((2, 3), 0, C, 1)
    prior((2, 3), 5 * C, C, 1)
    store(2, 2 * C, 2 * C).start()
    store(3, 0, C).start()
    store(4, 5 * C, C).start()

    first_sums(1)
    second_sums(1)
    for h in range(2):
        for q in range(4):

            @pl.when(jnp.logical_or(jnp.logical_or(h != xh, q != y), moved))
            def _():
                arrived(h, q).wait_recv()

    gram[...] = (fin[0].astype(F32) + fin[1].astype(F32)) * (-0.5 / (NP * 32))

    for copy in halos:
        copy.wait_send()
    for i in range(NC):
        to_sib(i).wait_send()
        to_far(i).wait_send()
        on(i).wait_send()
    for j in range(2):

        @pl.when(is_inner)
        def _():
            from_relay(0, j).wait_send()

    for d in (1, 2, 3):
        for k in range(4):
            gz(k, d).wait_send()
            gy(k, d).wait_send()
        for p in range(2):
            g2y(p, d).wait_send()
            g2z(p, d).wait_send()
    for h in range(2):
        for k in (1, 2, 3):
            to_result(h, k).wait_send()

        @pl.when(leaves(h))
        def _():
            to_result(h, 0).wait_send()

    for i, (start, size) in enumerate(((C, C), (4 * C, C), (2 * C, 2 * C), (0, C), (5 * C, C))):
        store(i, start, size).wait()


def finish(grad_in, gram_in, grad_out, gram_out, grad, gram, sem_in, sem_out):
    grad_rows = [pl.ds(r * C, C) for r in range(R)]
    loads = [pltpu.make_async_copy(grad_in.at[rows], grad.at[rows], sem_in.at[r]) for r, rows in enumerate(grad_rows)]
    loads.append(pltpu.make_async_copy(gram_in, gram, sem_in.at[R]))
    stores = [pltpu.make_async_copy(grad.at[rows], grad_out.at[rows], sem_out.at[r]) for r, rows in enumerate(grad_rows)]
    stores.append(pltpu.make_async_copy(gram, gram_out, sem_out.at[R]))
    for load in loads:
        load.start()
    for load, store in zip(loads, stores):
        load.wait()
        store.start()
    for store in stores:
        store.wait()


def shards(effects, kappa_sq, growth, tree_species, tree_counts, noise_precision, species_precision):
    vmem = pl.BlockSpec(memory_space=pltpu.VMEM)
    hbm = pl.BlockSpec(memory_space=pl.ANY)
    dma = pltpu.SemaphoreType.DMA
    grad, gram = pl.pallas_call(
        kernel,
        out_shape=(jax.ShapeDtypeStruct((NP, W), F32), jax.ShapeDtypeStruct((64, W), F32)),
        in_specs=[hbm, vmem, hbm, hbm, vmem, vmem, hbm],
        out_specs=(hbm, vmem),
        scratch_shapes=[
            pltpu.VMEM((NP, W), F32),
            pltpu.VMEM((NP, T), F32),
            pltpu.VMEM((NP, T), jnp.int32),
            pltpu.VMEM((4 * W, W), BF),
            pltpu.VMEM((NP, W), F32),
            pltpu.VMEM((2, C, W), F32),
            pltpu.VMEM((2, C, W), BF),
            pltpu.VMEM((2, C, W), BF),
            pltpu.VMEM((3 * C // 2, W), BF),
            pltpu.VMEM((R, C), F32),
            pltpu.VMEM((R, C), F32),
            pltpu.VMEM((8, C), F32),
            pltpu.VMEM((R + 2, C, T), F32),
            pltpu.VMEM((NP, T), jnp.int32),
            pltpu.VMEM((R + 2, C, W), F32),
            pltpu.VMEM((4, NP, W), BF),
            pltpu.VMEM((W, NP), BF),
            pltpu.VMEM((8 * C, T), F32),
            pltpu.VMEM((4, W, W), BF),
            pltpu.VMEM((2, W, W), F32),
            pltpu.VMEM((3, 4, 64, W), BF),
            pltpu.VMEM((3, 4, 256, T), BF),
            pltpu.VMEM((2, 4, 64, 2 * T), BF),
            pltpu.VMEM((2, 256, 2 * T), BF),
            pltpu.VMEM((2, 3, 64, 2 * T), BF),
            pltpu.VMEM((2, 3, 64, 2 * T), BF),
            pltpu.VMEM((2, 64, W), BF),
            pltpu.VMEM((2, 64, W), BF),
            dma((6,)), dma((6,)),
            dma((2,)), dma((2,)),
            dma((3, NC)), dma((3, NC)),
            dma((4, 3)), dma((4, 3)),
            dma((4, 3)), dma((4, 3)),
            dma((2, 3)), dma((2, 3)),
            dma((2, 3)), dma((2, 3)),
            dma((2, 4)), dma((2, 4)),
            dma((R + 3,)),
            dma((5,)),
        ],
        compiler_params=pltpu.CompilerParams(
            collective_id=0, has_side_effects=True, vmem_limit_bytes=56 << 20
        ),
        cost_estimate=pl.CostEstimate(flops=7_000_000_000, bytes_accessed=12_000_000, transcendentals=0),
        name="posterior_gradient",
    )(
        effects.reshape(NP, W),
        kappa_sq,
        growth.reshape(NP, T),
        tree_species.reshape(NP, T),
        tree_counts,
        noise_precision.reshape(1, W),
        species_precision,
    )
    grad, gram = pl.pallas_call(
        finish,
        out_shape=(jax.ShapeDtypeStruct((NP, W), F32), jax.ShapeDtypeStruct((64, W), F32)),
        in_specs=[hbm, hbm],
        out_specs=(hbm, hbm),
        scratch_shapes=[pltpu.VMEM((NP, W), F32), pltpu.VMEM((64, W), F32), dma((R + 1,)), dma((R + 1,))],
        compiler_params=pltpu.CompilerParams(vmem_limit_bytes=56 << 20),
        name="finish",
    )(grad, gram)
    return grad.reshape(R, C, W), gram


def solution(mesh):
    return jax.shard_map(
        shards,
        mesh=mesh,
        in_specs=(
            P("space", None, "species"),
            P("space", None),
            P("space", None, None),
            P("space", None, None),
            P("space", None),
            P("species"),
            P(None, "species"),
        ),
        out_specs=(P("space", None, "species"), P("space", "species")),
        check_vma=False,
    )
```

profile of v0, /device:TPU:3, one launch (start us, length us, event | category | flops | bytes accessed | tf_op | source)
XLA Modules:
  0.0 77.7 jit_solution(9278915005588784007)
XLA Ops:
  0.6 74.2 %posterior_gradient.1 = (f32[1536,512]{1,0:T(8,128)}, f32[64,512]{1,0:T(8,128)}) custom-call(f32[1536,512]{1,0:T(8,128)} %bitcast.5, f32[6,256]{1,0:T(8,128)} %kap.1, f32[1536,128]{1,0:T(8,128)} %bitcast.7, s32[1536,128]{1,0:T(8,128)} %bitcast.8, s32[6,256]{1,0:T(8,128)} %counts.1, f32[1,512]{1,0:T(1,128)} %bitcast.9, bf16[2048,512]{1,0:T(8,128)(2,1)} %prec_in.1), custom_call_target="tpu_custom_call" | custom-call | flops 7000000000 | bytes 12000000 | tf_op jit(solution)/shard_map/posterior_gradient/pallas_call | solution.py:551
  74.9 2.9 %finish.1 = (f32[1536,512]{1,0:T(8,128)}, f32[64,512]{1,0:T(8,128)}) custom-call(f32[1536,512]{1,0:T(8,128)} %get-tuple-element.6.grad_in, f32[64,512]{1,0:T(8,128)} %get-tuple-element.7.gram_in), custom_call_target="tpu_custom_call" | custom-call | tf_op jit(solution)/shard_map/finish/pallas_call | solution.py:610
where the time goes:
time: 77.9 us; the launch traced here: 77.7 us
  Pallas kernels  77.1 us (99%)
    pallas_call x1, Pallas kernels, shards(): pl.pallas_call(kernel, out_shape=(jax.ShapeDtypeStruct((NP, W), F32), jax...  74.2 us
    pallas_call x1, Pallas kernels, shards(): pl.pallas_call(finish, out_shape=(jax.ShapeDtypeStruct((NP, W), F32), jax...  2.85 us

commit v1 on v0

--- a/solution.py
+++ b/solution.py
@@ -101,12 +101,7 @@
     ]
     for copy in halos[:4]:
         copy.start()
-    for i, r in enumerate((1, 4)):
-        loads[r].wait()
-        far_out[i] = eff[r * C : (r + 1) * C, :].astype(BF)
-        halos[4 + i].start()
-
-    for r in (2, 3, 0, 5):
+    for r in (1, 4, 2, 3, 0, 5):
         loads[r].wait()
 
     def erow(r):
@@ -389,11 +384,16 @@
         held[1, :, cs] = total.astype(BF)
         results(p, 1)
 
-    for r in (1, 2, 3, 4):
+    for r in (1, 2, 3):
         first_row(r)
     spat_row(2)
+    send(0, 1)
+    first_row(4)
     spat_row(3)
-    send(2, 0, 1)
+    send(2)
+    for i, r in enumerate((1, 4)):
+        far_out[i] = eff[r * C : (r + 1) * C, :].astype(BF)
+        halos[4 + i].start()
     tmp[0:R, :] = counts[...].astype(F32)
     cnt_cols = tmp[...].T
     for r in range(R):

time: 77.9 us -> 78 us (level)
  no operation moved by 1% of the time
where the time goes in v1:
time: 78 us; the launch traced here: 77.7 us
  Pallas kernels  77 us (99%)
    pallas_call x1, Pallas kernels, shards(): pl.pallas_call(kernel, out_shape=(jax.ShapeDtypeStruct((NP, W), F32), jax...  74.2 us
    pallas_call x1, Pallas kernels, shards(): pl.pallas_call(finish, out_shape=(jax.ShapeDtypeStruct((NP, W), F32), jax...  2.85 us

profile of v1, /device:TPU:3, one launch (start us, length us, event | category | flops | bytes accessed | tf_op | source)
XLA Modules:
  0.0 77.7 jit_solution(4443509415874261397)
XLA Ops:
  0.6 74.2 %posterior_gradient.1 = (f32[1536,512]{1,0:T(8,128)}, f32[64,512]{1,0:T(8,128)}) custom-call(f32[1536,512]{1,0:T(8,128)} %bitcast.5, f32[6,256]{1,0:T(8,128)} %kap.1, f32[1536,128]{1,0:T(8,128)} %bitcast.7, s32[1536,128]{1,0:T(8,128)} %bitcast.8, s32[6,256]{1,0:T(8,128)} %counts.1, f32[1,512]{1,0:T(1,128)} %bitcast.9, bf16[2048,512]{1,0:T(8,128)(2,1)} %prec_in.1), custom_call_target="tpu_custom_call" | custom-call | flops 7000000000 | bytes 12000000 | tf_op jit(solution)/shard_map/posterior_gradient/pallas_call | solution.py:551
  74.8 2.9 %finish.1 = (f32[1536,512]{1,0:T(8,128)}, f32[64,512]{1,0:T(8,128)}) custom-call(f32[1536,512]{1,0:T(8,128)} %get-tuple-element.6.grad_in, f32[64,512]{1,0:T(8,128)} %get-tuple-element.7.gram_in), custom_call_target="tpu_custom_call" | custom-call | tf_op jit(solution)/shard_map/finish/pallas_call | solution.py:610

commit v2 on v1

--- a/solution.py
+++ b/solution.py
@@ -11,7 +11,7 @@
 R, C, W, T = 6, 256, 512, 128
 NP = R * C
 GROUP = 32
-CHUNKS = ((2 * C, C // 2), (2 * C + C // 2, C // 2), (3 * C, C), (C, C), (4 * C, C), (0, C), (5 * C, C))
+CHUNKS = ((2 * C, C), (3 * C, C // 4), (3 * C + C // 4, 3 * C // 4), (C, C), (4 * C, C), (0, C), (5 * C, C))
 NC = len(CHUNKS)
 
 
@@ -268,7 +268,7 @@
     def gram_early(k):
         def body(i, carry):
             cs = pl.ds(pl.multiple_of(i * 256, 256), 256)
-            late[k - 2, :, cs] = gram_rows(k, (1,), 1, cs) + gram_rows(k, (3,), 2, cs)
+            late[k - 2, :, cs] = gram_rows(k, (1, 4), 1, cs)
             return carry
 
         lax.fori_loop(0, W // 256, body, 0)
@@ -276,7 +276,7 @@
     def gram_late(k):
         def body(i, carry):
             cs = pl.ds(pl.multiple_of(i * 256, 256), 256)
-            total = late[k - 2, :, cs] + gram_rows(k, (0, 2, 5), 1, cs)
+            total = late[k - 2, :, cs] + gram_rows(k, (2,), 2, cs) + gram_rows(k, (0, 5), 1, cs)
             part[k, :, cs] = total.astype(BF)
             return carry
 
@@ -387,10 +387,10 @@
     for r in (1, 2, 3):
         first_row(r)
     spat_row(2)
-    send(0, 1)
+    send(0)
     first_row(4)
     spat_row(3)
-    send(2)
+    send(2, 1)
     for i, r in enumerate((1, 4)):
         far_out[i] = eff[r * C : (r + 1) * C, :].astype(BF)
         halos[4 + i].start()

time: 78 us -> 77.8 us (level)
  no operation moved by 1% of the time
where the time goes in v2:
time: 77.8 us; the launch traced here: 77.6 us
  Pallas kernels  77 us (99%)
    pallas_call x1, Pallas kernels, shards(): pl.pallas_call(kernel, out_shape=(jax.ShapeDtypeStruct((NP, W), F32), jax...  74.1 us
    pallas_call x1, Pallas kernels, shards(): pl.pallas_call(finish, out_shape=(jax.ShapeDtypeStruct((NP, W), F32), jax...  2.85 us

profile of v2, /device:TPU:3, one launch (start us, length us, event | category | flops | bytes accessed | tf_op | source)
XLA Modules:
  0.0 77.6 jit_solution(10804740224423084746)
XLA Ops:
  0.6 74.1 %posterior_gradient.1 = (f32[1536,512]{1,0:T(8,128)}, f32[64,512]{1,0:T(8,128)}) custom-call(f32[1536,512]{1,0:T(8,128)} %bitcast.5, f32[6,256]{1,0:T(8,128)} %kap.1, f32[1536,128]{1,0:T(8,128)} %bitcast.7, s32[1536,128]{1,0:T(8,128)} %bitcast.8, s32[6,256]{1,0:T(8,128)} %counts.1, f32[1,512]{1,0:T(1,128)} %bitcast.9, bf16[2048,512]{1,0:T(8,128)(2,1)} %prec_in.1), custom_call_target="tpu_custom_call" | custom-call | flops 7000000000 | bytes 12000000 | tf_op jit(solution)/shard_map/posterior_gradient/pallas_call | solution.py:551
  74.7 2.9 %finish.1 = (f32[1536,512]{1,0:T(8,128)}, f32[64,512]{1,0:T(8,128)}) custom-call(f32[1536,512]{1,0:T(8,128)} %get-tuple-element.6.grad_in, f32[64,512]{1,0:T(8,128)} %get-tuple-element.7.gram_in), custom_call_target="tpu_custom_call" | custom-call | tf_op jit(solution)/shard_map/finish/pallas_call | solution.py:610
